TPU v7x, 256 devices: a whole 4x4x8 slice. The times are simulated.
256 devices in a mesh: ctx: 32 (over z, x), head: 8 (over y, core).
Axes of the slice: x: 4, y: 4, z: 8, core: 2. Of those that a mesh axis runs over, the one named last changes fastest.
Arguments:
- lin_q: bfloat16 [12288, 4096], P('ctx', 'head'), may hold values from -6 to 6
- lin_k: bfloat16 [12288, 4096], P('ctx', 'head'), may hold values from -6 to 6
- lin_v: bfloat16 [12288, 4096], P('ctx', 'head'), may hold values from -16 to 16
- lin_decay: float32 [12288, 32], P('ctx', 'head'), may hold values from 0 to 1
- soft_q: bfloat16 [12288, 4096], P('ctx', 'head'), may hold values from -6 to 6
- soft_k: bfloat16 [12288, 1024], P('ctx', 'head'), may hold values from -6 to 6
- soft_v: bfloat16 [12288, 1024], P('ctx', 'head'), may hold values from -6 to 6
Outputs:
- lin_out: float32 [12288, 4096], P('ctx', 'head')
- soft_out: float32 [12288, 4096], P('ctx', 'head')
All inputs are finite; a program needn't handle non-finite values.
Results may differ from a plain program's by a relative error of at most 0.004.
Values may be sent and summed in bfloat16 or wider, within the bound.
A program may use at most 64 MiB of HBM per device.

v0:
```python
import math

import jax
import jax.numpy as jnp
from jax import lax
from jax.sharding import PartitionSpec as P

HEAD_DIM = 128
HEADS_LIN = 32


NEG_LARGE = -1e30


def carried_in(part, axis, combine, identity):
    place = lax.axis_index(axis)
    gathered = jax.tree.map(lambda a: lax.all_gather(a, axis), part)
    state = jax.tree.map(lambda a, e: jnp.zeros_like(a) + jnp.asarray(e, a.dtype), part, identity)

    def one(hop, state):
        return combine(
            state, jax.tree.map(lambda a: lax.dynamic_index_in_dim(a, hop, 0, False), gathered)
        )

    return lax.fori_loop(0, place, one, state)


def lightning_local(lin_q, lin_k, lin_v, lin_decay):
    row_count = lin_q.shape[0]
    head_count = lin_decay.shape[1]
    q_heads = lin_q.reshape(row_count, head_count, HEAD_DIM)
    k_heads = lin_k.reshape(row_count, head_count, HEAD_DIM)
    v_heads = lin_v.reshape(row_count, head_count, HEAD_DIM)
    cumulative = jnp.cumsum(lin_decay, axis=0)
    scores = jnp.einsum("thd,shd->hts", q_heads, k_heads, preferred_element_type=jnp.float32)
    position_indices = jnp.arange(row_count, dtype=jnp.int32)
    causal = position_indices[:, None] >= position_indices[None, :]
    column_cum = jnp.transpose(cumulative)
    spread = column_cum[:, :, None] - column_cum[:, None, :]
    weights = jnp.where(causal[None], scores * jnp.exp(-jnp.maximum(spread, 0.0)), 0.0).astype(
        jnp.bfloat16
    )
    intra = jnp.einsum("hts,she->the", weights, v_heads, preferred_element_type=jnp.float32)
    final_cum = cumulative[-1]
    decay_gain = jnp.exp(-final_cum)
    scaled_keys = k_heads.astype(jnp.float32) * jnp.exp(cumulative - final_cum)[:, :, None]
    local_state = jnp.einsum(
        "shd,she->hde", scaled_keys, v_heads.astype(jnp.float32), precision=lax.Precision.HIGHEST
    )
    return (q_heads, intra, decay_gain, local_state, cumulative)


def combine_states(earlier, later):
    return (earlier[0] * later[0], later[0][:, None, None] * earlier[1] + later[1])


def attend_update(running, queries, query_pos, key_block, value_block, key_first):
    largest, prob_total, weighted = running
    score_scale = 1.0 / math.sqrt(HEAD_DIM)
    scores = (
        jnp.einsum("rkgd,skd->kgrs", queries, key_block, preferred_element_type=jnp.float32)
        * score_scale
    )
    key_pos = key_first + jnp.arange(key_block.shape[0], dtype=jnp.int32)
    visible = query_pos[:, None] >= key_pos[None, :]
    scores = jnp.where(visible, scores, NEG_LARGE)
    new_largest = jnp.maximum(largest, jnp.max(scores, axis=-1))
    exponents = jnp.where(visible, jnp.exp(scores - new_largest[..., None]), 0.0)
    factor = jnp.exp(largest - new_largest)
    prob_total = prob_total * factor + jnp.sum(exponents, axis=-1)
    weighted = weighted * factor[..., None] + jnp.einsum(
        "kgrs,skd->kgrd",
        exponents.astype(jnp.bfloat16),
        value_block,
        preferred_element_type=jnp.float32,
    )
    return (new_largest, prob_total, weighted)


def body(lin_q, lin_k, lin_v, lin_decay, soft_q, soft_k, soft_v):
    row_count = lin_q.shape[0]
    q_heads, intra, decay_gain, local_state, cumulative = lightning_local(
        lin_q, lin_k, lin_v, lin_decay
    )
    identity = (jnp.ones_like(decay_gain), jnp.zeros_like(local_state))
    state_in = carried_in((decay_gain, local_state), "ctx", combine_states, identity)[1]
    inter = jnp.einsum(
        "thd,hde->the", q_heads.astype(jnp.float32), state_in, precision=lax.Precision.HIGHEST
    )
    mixed = intra + jnp.exp(-cumulative)[:, :, None] * inter
    square_sum = lax.psum(jnp.sum(mixed * mixed, axis=(1, 2)), "head")
    mean_square = square_sum / (HEADS_LIN * HEAD_DIM)
    lin_out = (mixed * lax.rsqrt(mean_square + 1e-05)[:, None, None]).reshape(row_count, -1)
    kv_local = soft_k.shape[1] // HEAD_DIM
    q_local = soft_q.shape[1] // HEAD_DIM
    group_size = q_local // kv_local
    my_index = lax.axis_index("ctx")
    query_sets = [(soft_q, my_index * row_count + jnp.arange(row_count, dtype=jnp.int32))]
    prepared = [
        (queries.reshape(queries.shape[0], kv_local, group_size, HEAD_DIM), position_indices)
        for queries, position_indices in query_sets
    ]
    initial = tuple(
        (
            (
                jnp.full((kv_local, group_size, queries.shape[0]), NEG_LARGE, jnp.float32),
                jnp.zeros((kv_local, group_size, queries.shape[0]), jnp.float32),
                jnp.zeros((kv_local, group_size, queries.shape[0], HEAD_DIM), jnp.float32),
            )
            for queries, position_indices in prepared
        )
    )
    running = initial
    key_piece = lax.all_gather(soft_k, "ctx", axis=0, tiled=True)
    value_piece = lax.all_gather(soft_v, "ctx", axis=0, tiled=True)
    shard_count = key_piece.shape[0] // row_count
    key_shards = key_piece.reshape(shard_count, row_count, kv_local, HEAD_DIM)
    value_shards = value_piece.reshape(shard_count, row_count, kv_local, HEAD_DIM)

    def per_shard(current, shard_item):
        key_block, value_block, shard_number = shard_item
        key_first = shard_number * row_count
        updated = []
        for (queries, position_indices), group_state in zip(prepared, current):
            needed = key_first <= position_indices[-1]
            updated.append(
                lax.cond(
                    needed,
                    lambda state_now: attend_update(
                        state_now, queries, position_indices, key_block, value_block, key_first
                    ),
                    lambda state_now: state_now,
                    group_state,
                )
            )
        return (tuple(updated), None)

    running, _ = lax.scan(
        per_shard, running, (key_shards, value_shards, jnp.arange(shard_count, dtype=jnp.int32))
    )
    outputs = []
    for (queries, position_indices), (largest, prob_total, weighted) in zip(prepared, running):
        result = weighted / prob_total[..., None]
        outputs.append(
            jnp.transpose(result, (2, 0, 1, 3)).reshape(queries.shape[0], q_local * HEAD_DIM)
        )
    soft_out = outputs[0]
    return (lin_out, soft_out)


def solution(mesh):
    return jax.shard_map(
        body,
        mesh=mesh,
        in_specs=(
            P("ctx", "head"),
            P("ctx", "head"),
            P("ctx", "head"),
            P("ctx", "head"),
            P("ctx", "head"),
            P("ctx", "head"),
            P("ctx", "head"),
        ),
        out_specs=(P("ctx", "head"), P("ctx", "head")),
        check_vma=False,
    )
```

profile of v0, /device:TPU:231, one launch (start us, length us, event | category | flops | bytes accessed | tf_op | source)
XLA Modules:
  0.0 443.5 jit_solution(10317167620759667029)
XLA Ops:
  15.3 28.2 %all-gather.1 = f32[32,1,4]{2,1,0:T(1,128)S(1)} all-gather(f32[1,1,4]{2,1,0:T(1,128)S(1)} %bitcast.143), channel_id=1, replica_groups=mesh['ctx'=32,'head'=8] {'ctx'}, dimensions={0}, use_global_device_ids=true | all-gather | bytes 528 | tf_op jit(solution)/shard_map/all_gather | solution.py:17
  44.6 38.9 %all-gather.6.cloned.1.call-done = bf16[12288,128]{1,0:T(8,128)(2,1)} async-done(((bf16[384,128]{1,0:T(8,128)(2,1)}), bf16[12288,128]{1,0:T(8,128)(2,1)}) %all-gather.6.cloned.1.call-update) | async-done | bytes 3145744 | tf_op jit(solution)/shard_map/all_gather | solution.py:114
  83.5 79.1 %all-gather.8.cloned.1.call-done = bf16[12288,128]{1,0:T(8,128)(2,1)} async-done(((bf16[384,128]{1,0:T(8,128)(2,1)}), bf16[12288,128]{1,0:T(8,128)(2,1)}) %all-gather.8.cloned.1.call-update) | async-done | bytes 3145744 | tf_op jit(solution)/shard_map/all_gather | solution.py:115
  162.7 219.7 %while.27 = (s32[]{:T(128)}, f32[1,4,384]{2,1,0:T(4,128)S(1)}, f32[1,4,384]{2,1,0:T(4,128)S(1)}, f32[1,4,384,128]{3,2,1,0:T(8,128)S(1)}, s32[32]{0:T(128)S(1)}, ...) while((s32[]{:T(128)}, f32[1,4,384]{2,1,0:T(4,128)S(1)}, ...), condition=%wide.region_11.12_spmd, body=%wide.region_6.11_spmd.sunk | while | flops 310203264 | bytes 9934623 | solution.py:138
  179.1 4.3 conditional.2
  185.9 4.3 conditional.2
  192.8 4.3 conditional.2
  199.7 4.3 conditional.2
  206.5 4.3 conditional.2
  213.4 4.3 conditional.2
  220.2 4.3 conditional.2
  227.1 4.3 conditional.2
  234.0 4.3 conditional.2
  240.9 4.3 conditional.2
  247.8 4.3 conditional.2
  254.6 4.3 conditional.2
  288.9 4.3 conditional.2
  295.8 4.3 conditional.2
  302.7 4.3 conditional.2
  309.5 4.3 conditional.2
  316.4 4.3 conditional.2
  323.3 4.3 conditional.2
  384.2 34.4 %while.26 = (s32[]{:T(128)}, f32[4,128,128]{2,1,0:T(8,128)S(1)}, s32[]{:T(128)}, f32[32,4]{1,0:T(8,128)S(1)}, f32[32,4,128,128]{3,2,1,0:T(8,128)}, /*index=5*/s32[]{:T(128)}, s32[]{:T(128)}, s32[]{:T(128)}) while((s32[]{:T(128)}, f32[4,128,128]{2,1,0:T(8,128)S(1)}, s32[]{:T(128)}, f32[32,4]{1,0:T(8,128)S(1)}, f32[32,4,128,128]{3,2,1,0:T(8,128)}, ...), condition=%wide.region_3.4_spmd, body=%wide.region_2.3_spmd.sunk | while | flops 131077 | bytes 786607 | solution.py:25
  419.2 16.6 %psum.7 = f32[384]{0:T(512)S(1)} all-reduce(f32[384]{0:T(512)S(1)} %get-tuple-element.271), channel_id=1, replica_groups=mesh['ctx'=32,'head'=8] {'head'}, use_global_device_ids=true, to_apply=%region_5.6 | all-reduce | flops 384 | bytes 3072 | tf_op jit(solution)/shard_map/psum | solution.py:91
  (436 shorter events, 280.2 us)
Async XLA Ops:
  7.2 36.4 %copy-start = (bf16[384,512]{1,0:T(8,128)(2,1)S(1)}, bf16[384,512]{1,0:T(8,128)(2,1)}, u32[]{:S(2)}) copy-start(bf16[384,512]{1,0:T(8,128)(2,1)} %param.13) | copy-start | bytes 1179652
  7.2 36.3 %copy-start.2 = (bf16[384,512]{1,0:T(8,128)(2,1)S(1)}, bf16[384,512]{1,0:T(8,128)(2,1)}, u32[]{:S(2)}) copy-start(bf16[384,512]{1,0:T(8,128)(2,1)} %param.15) | copy-start | bytes 1179652
  7.2 7.6 %copy-start.1 = (bf16[384,512]{1,0:T(8,128)(2,1)S(1)}, bf16[384,512]{1,0:T(8,128)(2,1)}, u32[]{:S(2)}) copy-start(bf16[384,512]{1,0:T(8,128)(2,1)} %param.17) | copy-start | bytes 1179652
  7.2 76.3 %all-gather.6.cloned.1.call-start = ((), (), s32[]{:S(2)}) async-start(), calls=%async_computation | async-start | bytes 3244032 | tf_op jit(solution)/shard_map/all_gather | solution.py:114
  7.9 154.7 %all-gather.8.cloned.1.call-start = ((), (), s32[]{:S(2)}) async-start(), calls=%async_computation.1 | async-start | bytes 3244032 | tf_op jit(solution)/shard_map/all_gather | solution.py:115
  8.7 375.5 %all-gather.10.cloned.1.call-start = ((), (), s32[]{:S(2)}) async-start(), calls=%async_computation.2 | async-start | bytes 8650752 | tf_op jit(solution)/shard_map/all_gather | solution.py:17
Sparse Core Ops, SparseCore 0:
  10.6 72.8 all-gather.5
  86.1 76.5 all-gather.7
  165.8 98.3 all-gather.9
where the time goes:
time: 447 us; the launch traced here: 444 us
  waiting for transfers between devices  119 us (27%)
  matrix products  113 us (25%)
  other arithmetic  59.8 us (13%)
  loops' own time  46.2 us (10%)
  local copies, waits for them, and re-layouts  45.9 us (10%)
  blocking collectives  44.7 us (10%)
  between operations  13.9 us (3%)
    all_gather x1, waiting for transfers between devices, body(): value_piece = lax.all_gather(soft_v, 'ctx', axis=0, tiled=True)  79.1 us
    dot_general x32, matrix products, attend_update(): jnp.einsum('kgrs,skd->kgrd', exponents.astype(jnp.bfloat16), value_block,...  62.7 us
    dot_general x32, matrix products, attend_update(): jnp.einsum('rkgd,skd->kgrs', queries, key_block, preferred_element_type=j...  46.8 us
    another operation x1, loops' own time, body(): lax.scan(per_shard, running, (key_shards, value_shards, jnp.arange(shard_...  43.2 us
    all_gather x1, waiting for transfers between devices, body(): key_piece = lax.all_gather(soft_k, 'ctx', axis=0, tiled=True)  38.9 us
    add x31, other arithmetic, combine_states(): later[0][:, None, None] * earlier[1] + later[1]  32.9 us
    all_gather x1, blocking collectives, carried_in(): gathered = jax.tree.map(lambda a: lax.all_gather(a, axis), part)  28.2 us
    dynamic_slice x32, local copies, waits for them, and re-layouts, body(): lax.scan(per_shard, running, (key_shards, value_shards, jnp.arange(shard_...  21.4 us
  transfers between devices with their start and end apart: 3, of which 2 were waited for; matrix products, arithmetic and copies ran while one was open for 41% of the time, Pallas kernels for 0%

commit v1 on v0

v1 whole, which is shorter than its diff:
```python
import math

import jax
import jax.numpy as jnp
from jax import lax
from jax.experimental import pallas as pl
from jax.experimental.pallas import tpu as pltpu
from jax.sharding import PartitionSpec as P

MESH = pl.DeviceIdType.MESH
F32 = jnp.float32
BF16 = jnp.bfloat16
D = 128
R = 384
NX = 4
NZ = 8
NH = 4
MODEL = 4096
HIGHEST = lax.Precision.HIGHEST
SCALE = math.log2(math.e) / math.sqrt(D)
START = -1e30
HIDDEN = -2e30

A_BT = (((1,), (1,)), ((), ()))


def dot(a, b):
    return jnp.dot(a, b, preferred_element_type=F32)


def split(a):
    high = a.astype(BF16)
    return high, (a - high.astype(F32)).astype(BF16)


def kernel(
    lq, lk, lv, ld, sq, sk, sv, lin_out, soft_out,
    kb, vb, qb, acc, mx, ob, ls, orv, lrv,
    mixed, cums, p1s, p1r, p2r, p3s, p3r, ssr,
    k_rs, v_rs, k_ss, v_ss, q_rs, q_ss, o_rs, o_ss, l_rs, l_ss,
    p1_rs, p1_ss, p2_rs, p2_ss, p3_rs, p3_ss, s_rs, s_ss,
):
    c = lax.axis_index("ctx")
    hd = lax.axis_index("head")
    z = c // NX
    x = c % NX

    def at_z(dz):
        return (lax.rem(z + dz + NZ, NZ) * NX + x, hd)

    def at_x(dx):
        return (z * NX + lax.rem(x + dx + NX, NX), hd)

    def at_h(dh):
        return (c, lax.rem(hd + dh, 8))

    def rows(r):
        return pl.ds(pl.multiple_of(r * R, R), R)

    def row_of(dz):
        return lax.rem(z + dz + NZ, NZ)

    def remote(src, dst, ss, rs, dev):
        return pltpu.make_async_remote_copy(
            src_ref=src, dst_ref=dst, send_sem=ss, recv_sem=rs, device_id=dev, device_id_type=MESH
        )

    def k_copy(dz, way):
        r = row_of(dz)
        n = 0 if dz == 0 and way > 0 else (1 if dz == 0 else (1 + abs(dz) if way > 0 else 4 + abs(dz)))
        return remote(kb.at[rows(r), :], kb.at[rows(r), :], k_ss.at[n], k_rs.at[r], at_z(way))

    def v_copy(dz, way):
        r = row_of(dz)
        n = 0 if dz == 0 and way > 0 else (1 if dz == 0 else (1 + abs(dz) if way > 0 else 4 + abs(dz)))
        part = vb.at[pl.ds(0, D), rows(r)]
        return remote(part, part, v_ss.at[n], v_rs.at[r], at_z(way))

    k_sends = [(0, 1), (0, -1), (-1, 1), (1, -1), (-2, 1), (2, -1), (-3, 1)]
    v_sends = [(0, 1), (0, -1), (-1, 1), (1, -1), (-2, 1), (2, -1), (3, -1)]

    def tile_of(slot, h):
        return h if slot == 0 else (4 + 2 * h if slot == 1 else (5 + 2 * h if slot == 2 else 12 + h))

    def q_copy(slot, h):
        t = tile_of(slot, h)
        dx = {1: -1, 2: 1, 3: 2}[slot]
        return remote(
            sq.at[:, pl.ds(h * D, D)], qb.at[t], q_ss.at[t - 4], q_rs.at[t - 4], at_x(dx)
        )

    def o_copy(slot, h, count):
        dx = {1: 1, 2: -1, 3: 2}[slot]
        part = pl.ds(h, count)
        n = 2 * (slot - 1) + h // 2
        return remote(
            ob.at[slot - 1, part], orv.at[slot - 1, part], o_ss.at[n], o_rs.at[n], at_x(dx)
        )

    def l_copy(slot):
        dx = {1: 1, 2: -1, 3: 2}[slot]
        return remote(
            ls.at[slot - 1], lrv.at[slot - 1], l_ss.at[slot - 1], l_rs.at[slot - 1], at_x(dx)
        )

    def p1_copy(dx):
        there = lax.rem(x + dx, NX)
        return remote(p1s.at[there], p1r.at[x], p1_ss.at[dx], p1_rs.at[x], at_x(dx))

    def p1_wait(dx):
        there = lax.rem(x + dx, NX)
        remote(p1s.at[there], p1r.at[there], p1_ss.at[dx], p1_rs.at[there], at_x(dx)).wait_recv()

    def p2_copy(dz):
        return remote(p2r.at[z], p2r.at[z], p2_ss.at[dz], p2_rs.at[z], at_z(dz))

    def p2_wait(dz):
        r = z - dz
        remote(p2r.at[r], p2r.at[r], p2_ss.at[dz], p2_rs.at[r], at_z(dz)).wait_recv()

    def p3_copy(dx):
        there = lax.rem(x + dx, NX)
        return remote(p3s.at[there], p3r.at[x], p3_ss.at[dx], p3_rs.at[x], at_x(dx))

    def p3_wait(dx):
        there = lax.rem(x + dx, NX)
        remote(p3s.at[there], p3r.at[there], p3_ss.at[dx], p3_rs.at[there], at_x(dx)).wait_recv()

    def s_copy(dh):
        return remote(ssr.at[hd], ssr.at[hd], s_ss.at[dh], s_rs.at[hd], at_h(dh))

    def s_wait(dh):
        there = lax.rem(hd + dh, 8)
        remote(ssr.at[there], ssr.at[there], s_ss.at[dh], s_rs.at[there], at_h(dh)).wait_recv()

    barrier = pltpu.get_barrier_semaphore()
    for dz in range(1, NZ):
        pl.semaphore_signal(barrier, inc=1, device_id=at_z(dz), device_id_type=MESH)
    for dx in range(1, NX):
        pl.semaphore_signal(barrier, inc=1, device_id=at_x(dx), device_id_type=MESH)
    for dh in range(1, 8):
        pl.semaphore_signal(barrier, inc=1, device_id=at_h(dh), device_id_type=MESH)

    kb[rows(z), :] = sk[...]
    vb[pl.ds(0, D), rows(z)] = sv[...].T
    vb[pl.ds(D, 16), :] = jnp.ones((16, NZ * R), BF16)
    for h in range(NH):
        qb[h] = sq[:, h * D : (h + 1) * D]
    pl.semaphore_wait(barrier, 17)

    for way in (1, -1):
        k_copy(0, way).start()
        v_copy(0, way).start()
    for h in range(NH):
        q_copy(1, h).start()
        q_copy(2, h).start()
    for h in range(NH):
        q_copy(3, h).start()

    t_at = lax.broadcasted_iota(jnp.int32, (R, R), 0)
    s_at = lax.broadcasted_iota(jnp.int32, (R, R), 1)
    causal = t_at >= s_at
    cum = jnp.dot(causal.astype(F32), ld[...], precision=HIGHEST, preferred_element_type=F32)
    cum = jnp.concatenate([cum, jnp.zeros((R, D - NH), F32)], axis=1)
    cums[...] = cum
    cum_row = cum.T
    for h in range(NH):
        cols = slice(h * D, (h + 1) * D)
        qh, kh, vh = lq[:, cols], lk[:, cols], lv[:, cols]
        cum_t = cum[:, h : h + 1]
        cum_s = cum_row[h : h + 1, :]
        last = cum[R - 1 : R, h : h + 1]
        scores = lax.dot_general(qh, kh, A_BT, preferred_element_type=F32)
        weights = jnp.where(causal, scores * jnp.exp(-jnp.maximum(cum_t - cum_s, 0.0)), 0.0)
        mixed[:, cols] = dot(weights.astype(BF16), vh)
        scaled = kh.astype(F32) * jnp.exp(cum_t - last)
        high, low = split(scaled)
        p1s[h, 0:D, :] = dot(high.T, vh) + dot(low.T, vh)
        p1s[h, D : D + 8, :] = jnp.broadcast_to(last, (8, D))
    for dx in range(1, NX):
        p1_copy(dx).start()
    p1r[x] = p1s[x]

    for_all = jnp.full((8, R), START, F32)
    for t in range(16):
        mx[t] = for_all
        acc[t] = jnp.zeros((D + 16, R), F32)

    diff = s_at - t_at

    def block(i, base, size, masked):
        sub = 768 if size == 768 else 512
        parts = size // sub

        def score(j):
            q = qb[4 * i + j]
            out = []
            for n in range(parts):
                keys = kb[pl.ds(pl.multiple_of(base + n * sub, R if sub == 768 else D), sub), :]
                out.append(lax.dot_general(keys, q, A_BT, preferred_element_type=F32))
            return out

        def finish(j, ps, al):
            total = acc[4 * i + j] * al
            for n in range(parts):
                values = vb[:, pl.ds(pl.multiple_of(base + n * sub, D), sub)]
                total = total + dot(values, ps[n])
            acc[4 * i + j] = total

        now = score(0)
        pending = None
        for j in range(4):
            later = score(j + 1) if j < 3 else None
            if pending is not None:
                finish(*pending)
            if masked:
                dx = jnp.where(i == 0, 0, jnp.where(i == 3, 2, 1 if j % 2 == 0 else -1))
                there = lax.rem(x + dx + NX, NX)
                first = base // R
                halves = []
                for half in range(2):
                    lead = (NX * (z - first - half) + there - x) * R
                    seen = diff + lead >= 0
                    halves.append(jnp.where(seen, now[0][half * R : (half + 1) * R], HIDDEN))
                now = halves
            top = now[0].max(axis=0, keepdims=True)
            for n in range(1, len(now)):
                top = jnp.maximum(top, now[n].max(axis=0, keepdims=True))
            old = mx[4 * i + j, 0:1, :]
            new = jnp.maximum(old, top * SCALE)
            al = jnp.exp2(old - new)
            mx[4 * i + j, 0:1, :] = new
            ps = [jnp.exp2(s * SCALE - new).astype(BF16) for s in now]
            if masked:
                ps = [jnp.concatenate(ps, axis=0)]
            pending = (j, ps, al)
            now = later
        finish(*pending)

    def closed(t):
        l = jnp.maximum(acc[t, D : D + 1, :], 1e-35)
        return acc[t, 0:D, :] / l, mx[t, 0:1, :] + jnp.log2(l)

    def close(slot, heads):
        for h in heads:
            o, lse = closed(tile_of(slot, h))
            ob[slot - 1, h] = o.astype(BF16)
            ls[slot - 1, h : h + 1, :] = lse

    def lin_totals():
        for dx in range(1, NX):
            p1_wait(dx)
        total = p1r[0, 0:D, :]
        lead = p1r[0, D : D + 8, :]
        for n in range(1, NX):
            g = p1r[n, D : D + 8, :]
            total = total * jnp.exp(-g[0:1]) + p1r[n, 0:D, :]
            lead = lead + g
        p2r[z, 0:D, :] = total
        p2r[z, D : D + 8, :] = lead
        for dz in range(1, NZ):
            @pl.when(z + dz < NZ)
            def _():
                p2_copy(dz).start()

    def lin_prefix():
        p3s[0] = jnp.zeros((D, D), F32)
        for dz in range(NZ - 1, 0, -1):
            @pl.when(z - dz >= 0)
            def _():
                p2_wait(dz)
                r = z - dz
                g = p2r[r, D : D + 8, :]
                p3s[0] = p3s[0] * jnp.exp(-g[0:1]) + p2r[r, 0:D, :]

        for n in range(1, NX):
            g = p1r[n - 1, D : D + 8, :]
            p3s[n] = p3s[n - 1] * jnp.exp(-g[0:1]) + p1r[n - 1, 0:D, :]
        for dx in range(1, NX):
            p3_copy(dx).start()
        p3r[x] = p3s[x]

    def lin_mix():
        for dx in range(1, NX):
            p3_wait(dx)
        square = jnp.zeros((R, D), F32)
        for h in range(NH):
            cols = slice(h * D, (h + 1) * D)
            high, low = split(p3r[h])
            qh = lq[:, cols]
            inter = dot(qh, high) + dot(qh, low)
            m = mixed[:, cols] + jnp.exp(-cums[:, h : h + 1]) * inter
            mixed[:, cols] = m
            square = square + m * m
        ssr[hd] = lax.dot_general(
            jnp.ones((8, D), F32), square, A_BT, precision=HIGHEST, preferred_element_type=F32
        )
        for dh in range(1, 8):
            s_copy(dh).start()

    def z_step(d):
        if d < 4:
            wait_k(-d)
            wait_v(-d)
            wait_k(d)
            wait_v(d)
        else:
            wait_k(4)
            wait_v(4)
        for dz, way in k_sends:
            if abs(dz) == d:
                k_copy(dz, way).start()
        for dz, way in v_sends:
            if abs(dz) == d:
                v_copy(dz, way).start()

    def wait_k(dz):
        r = row_of(dz)
        part = kb.at[rows(r), :]
        remote(part, part, k_ss.at[0], k_rs.at[r], at_z(1)).wait_recv()

    def wait_v(dz):
        r = row_of(dz)
        part = vb.at[pl.ds(0, D), rows(r)]
        remote(part, part, v_ss.at[0], v_rs.at[r], at_z(1)).wait_recv()

    own = 2 * (z // 2) * R

    def step(n, carry):
        is_a = (n <= 2) | (n == 6)
        is_b = ((n >= 3) & (n <= 5)) | (n == 7)
        i = jnp.where(
            n <= 2, n, jnp.where(n <= 5, n - 3, jnp.where(n <= 8, 3, jnp.where(n == 11, 0, n - 8)))
        )

        @pl.when(n == 0)
        def _():
            z_step(1)

        @pl.when(n == 1)
        def _():
            for h in (0, 1):
                q_copy(1, h).wait_recv()
                q_copy(2, h).wait_recv()

        @pl.when(n == 2)
        def _():
            z_step(2)
            lin_totals()
            for h in (2, 3):
                q_copy(1, h).wait_recv()
                q_copy(2, h).wait_recv()

        @pl.when(n == 5)
        def _():
            z_step(3)
            lin_prefix()

        @pl.when(n == 6)
        def _():
            for h in range(NH):
                q_copy(3, h).wait_recv()

        @pl.when(n == 8)
        def _():
            z_step(4)
            lin_mix()

        @pl.when(is_a)
        def _():
            block(i, own, 768, True)

        @pl.when(is_b & ((z == 7) | ((z % 2 == 0) & (z > 0))))
        def _():
            block(i, jnp.where(z == 7, 0, (z - 2) * R), 768, False)

        @pl.when((n >= 8) & (z >= 5))
        def _():
            block(i, jnp.where(z == 7, 2 * R, 0), 1536, False)

        @pl.when((n >= 8) & ((z == 3) | (z == 4)))
        def _():
            block(i, 0 * z, 768, False)

        @pl.when(n == 8)
        def _():
            close(3, range(NH))
            l_copy(3).start()
            o_copy(3, 0, 2).start()
            o_copy(3, 2, 2).start()

        @pl.when(n == 9)
        def _():
            for slot in (1, 2):
                close(slot, (0, 1))
                o_copy(slot, 0, 2).start()

        @pl.when(n == 10)
        def _():
            for slot in (1, 2):
                close(slot, (2, 3))
                o_copy(slot, 2, 2).start()
                l_copy(slot).start()

        return carry

    lax.fori_loop(0, 12, step, 0)

    for dh in range(1, 8):
        s_wait(dh)
    square = ssr[0]
    for n in range(1, 8):
        square = square + ssr[n]
    scale = lax.rsqrt(square[0:1, :] * (1.0 / MODEL) + 1e-05)
    scale = jnp.broadcast_to(scale, (D, R)).T
    for h in range(NH):
        cols = slice(h * D, (h + 1) * D)
        lin_out[:, cols] = mixed[:, cols] * scale

    for slot in (3, 1, 2):
        l_copy(slot).wait_recv()
    for h in range(NH):
        if h % 2 == 0:
            for slot in (3, 1, 2):
                o_copy(slot, h, 2).wait_recv()
        o, lse = closed(h)
        others = [lrv[n, h : h + 1, :] for n in range(3)]
        top = lse
        for one in others:
            top = jnp.maximum(top, one)
        w = jnp.exp2(lse - top)
        total = w
        o = o * w
        for n in range(3):
            w = jnp.exp2(others[n] - top)
            total = total + w
            o = o + orv[n, h].astype(F32) * w
        soft_out[:, h * D : (h + 1) * D] = (o / total).T

    for dz, way in k_sends:
        k_copy(dz, way).wait_send()
    for dz, way in v_sends:
        v_copy(dz, way).wait_send()
    for slot in (1, 2, 3):
        for h in range(NH):
            q_copy(slot, h).wait_send()
        for h in (0, 2):
            o_copy(slot, h, 2).wait_send()
        l_copy(slot).wait_send()
    for dx in range(1, NX):
        p1_copy(dx).wait_send()
        p3_copy(dx).wait_send()
    for dz in range(1, NZ):
        @pl.when(z + dz < NZ)
        def _():
            p2_copy(dz).wait_send()
    for dh in range(1, 8):
        s_copy(dh).wait_send()


def body(lin_q, lin_k, lin_v, lin_decay, soft_q, soft_k, soft_v):
    dma = pltpu.SemaphoreType.DMA
    vmem = pl.BlockSpec(memory_space=pltpu.VMEM)
    out = jax.ShapeDtypeStruct((R, NH * D), F32)
    return pl.pallas_call(
        kernel,
        out_shape=(out, out),
        in_specs=[vmem] * 7,
        out_specs=(vmem, vmem),
        scratch_shapes=[
            pltpu.VMEM((NZ * R, D), BF16),
            pltpu.VMEM((D + 16, NZ * R), BF16),
            pltpu.VMEM((16, R, D), BF16),
            pltpu.VMEM((16, D + 16, R), F32),
            pltpu.VMEM((16, 8, R), F32),
            pltpu.VMEM((3, NH, D, R), BF16),
            pltpu.VMEM((3, 8, R), F32),
            pltpu.VMEM((3, NH, D, R), BF16),
            pltpu.VMEM((3, 8, R), F32),
            pltpu.VMEM((R, NH * D), F32),
            pltpu.VMEM((R, D), F32),
            pltpu.VMEM((NX, D + 8, D), F32),
            pltpu.VMEM((NX, D + 8, D), F32),
            pltpu.VMEM((NZ, D + 8, D), F32),
            pltpu.VMEM((NX, D, D), F32),
            pltpu.VMEM((NX, D, D), F32),
            pltpu.VMEM((8, 8, R), F32),
            dma((8,)), dma((8,)), dma((8,)), dma((8,)),
            dma((12,)), dma((12,)), dma((6,)), dma((6,)), dma((3,)), dma((3,)),
            dma((4,)), dma((4,)), dma((8,)), dma((8,)), dma((4,)), dma((4,)), dma((8,)), dma((8,)),
        ],
        compiler_params=pltpu.CompilerParams(
            collective_id=0, has_side_effects=True, vmem_limit_bytes=48 << 20
        ),
    )(lin_q, lin_k, lin_v, lin_decay, soft_q, soft_k, soft_v)


def solution(mesh):
    spec = P("ctx", "head")
    return jax.shard_map(
        body, mesh=mesh, in_specs=(spec,) * 7, out_specs=(spec, spec), check_vma=False
    )
```

time: 447 us -> 78.5 us (0.18)
  the two profiles are of different devices: /device:TPU:231 before, /device:TPU:224 now
where the time goes in v1:
time: 78.5 us; the launch traced here: 77.9 us
  Pallas kernels  70.5 us (90%)
  local copies, waits for them, and re-layouts  6.67 us (8%)
    pallas_call x1, Pallas kernels, body(): pl.pallas_call(kernel, out_shape=(out, out), in_specs=[vmem] * 7, out_spe...  70.5 us
    unnamed x15, local copies, waits for them, and re-layouts  6.67 us

profile of v1, /device:TPU:224, one launch (start us, length us, event | category | flops | bytes accessed | tf_op | source)
XLA Modules:
  0.0 77.9 jit_solution(7479274208881900428)
XLA Ops:
  0.6 0.0 copy-start.5
  0.6 0.0 copy-start.4
  0.7 0.9 %copy.9.ld = f32[384,4]{1,0:T(8,128)S(1)} copy(f32[384,4]{0,1:T(4,128)} %param.10) | data formatting | bytes 12288 | tf_op args[3]
  1.5 0.0 copy-done.5
  1.5 0.1 copy-done.4
  1.6 0.0 copy-start
  1.6 1.0 %copy-done = bf16[384,512]{1,0:T(8,128)(2,1)S(1)} copy-done((bf16[384,512]{1,0:T(8,128)(2,1)S(1)}, bf16[384,512]{1,0:T(8,128)(2,1)}, u32[]{:S(2)}) %copy-start) | copy-done | bytes 393240
  2.6 0.0 copy-start.1
  2.6 1.0 %copy-done.1 = bf16[384,512]{1,0:T(8,128)(2,1)S(1)} copy-done((bf16[384,512]{1,0:T(8,128)(2,1)S(1)}, bf16[384,512]{1,0:T(8,128)(2,1)}, u32[]{:S(2)}) %copy-start.1) | copy-done | bytes 393240
  3.6 0.0 copy-start.2
  3.6 1.0 %copy-done.2 = bf16[384,512]{1,0:T(8,128)(2,1)S(1)} copy-done((bf16[384,512]{1,0:T(8,128)(2,1)S(1)}, bf16[384,512]{1,0:T(8,128)(2,1)}, u32[]{:S(2)}) %copy-start.2) | copy-done | bytes 393240
  4.6 0.0 copy-start.3
  4.6 1.0 %copy-done.3 = bf16[384,512]{1,0:T(8,128)(2,1)S(1)} copy-done((bf16[384,512]{1,0:T(8,128)(2,1)S(1)}, bf16[384,512]{1,0:T(8,128)(2,1)}, u32[]{:S(2)}) %copy-start.3) | copy-done | bytes 393240
  5.6 70.5 %shard_map.86 = (f32[384,512]{1,0:T(8,128)S(1)}, f32[384,512]{1,0:T(8,128)S(1)}) custom-call(bf16[384,512]{1,0:T(8,128)(2,1)S(1)} %copy-done, bf16[384,512]{1,0:T(8,128)(2,1)S(1)} %copy-done.1, bf16[384,512]{1,0:T(8,128)(2,1)S(1)} %copy-done.2, f32[384,4]{1,0:T(8,128)S(1)} %copy.9.ld, bf16[384,512]{1,0:T(8,128)(2,1)S(1)} %copy-done.3, ...), custom_call_target="tpu_custom_call" | custom-call | tf_op jit(solution)/shard_map/pallas_call | solution.py:465
  76.1 0.9 %copy.12 = f32[384,512]{1,0:T(8,128)} copy(f32[384,512]{1,0:T(8,128)S(1)} %get-tuple-element.4) | data formatting | bytes 1572864
  77.0 0.9 %copy.13 = f32[384,512]{1,0:T(8,128)} copy(f32[384,512]{1,0:T(8,128)S(1)} %get-tuple-element.5) | data formatting | bytes 1572864
Async XLA Ops:
  0.6 0.9 %copy-start.5 = (bf16[384,128]{1,0:T(8,128)(2,1)S(1)}, bf16[384,128]{1,0:T(8,128)(2,1)}, u32[]{:S(2)}) copy-start(bf16[384,128]{1,0:T(8,128)(2,1)} %sv.1) | copy-start | bytes 294916
  0.6 0.9 %copy-start.4 = (bf16[384,128]{1,0:T(8,128)(2,1)S(1)}, bf16[384,128]{1,0:T(8,128)(2,1)}, u32[]{:S(2)}) copy-start(bf16[384,128]{1,0:T(8,128)(2,1)} %sk.1) | copy-start | bytes 294916
  1.6 1.0 %copy-start = (bf16[384,512]{1,0:T(8,128)(2,1)S(1)}, bf16[384,512]{1,0:T(8,128)(2,1)}, u32[]{:S(2)}) copy-start(bf16[384,512]{1,0:T(8,128)(2,1)} %lq.1) | copy-start | bytes 1179652
  2.6 1.0 %copy-start.1 = (bf16[384,512]{1,0:T(8,128)(2,1)S(1)}, bf16[384,512]{1,0:T(8,128)(2,1)}, u32[]{:S(2)}) copy-start(bf16[384,512]{1,0:T(8,128)(2,1)} %lk.1) | copy-start | bytes 1179652
  3.6 1.0 %copy-start.2 = (bf16[384,512]{1,0:T(8,128)(2,1)S(1)}, bf16[384,512]{1,0:T(8,128)(2,1)}, u32[]{:S(2)}) copy-start(bf16[384,512]{1,0:T(8,128)(2,1)} %lv.1) | copy-start | bytes 1179652
  4.6 1.0 %copy-start.3 = (bf16[384,512]{1,0:T(8,128)(2,1)S(1)}, bf16[384,512]{1,0:T(8,128)(2,1)}, u32[]{:S(2)}) copy-start(bf16[384,512]{1,0:T(8,128)(2,1)} %sq.1) | copy-start | bytes 1179652

commit v2 on v1

v2 whole, which is shorter than its diff:
```python
import math

import jax
import jax.numpy as jnp
from jax import lax
from jax.experimental import pallas as pl
from jax.experimental.pallas import tpu as pltpu
from jax.sharding import PartitionSpec as P

MESH = pl.DeviceIdType.MESH
F32 = jnp.float32
BF16 = jnp.bfloat16
D = 128
R = 384
NX = 4
NZ = 8
NH = 4
MODEL = 4096
HIGHEST = lax.Precision.HIGHEST
SCALE = math.log2(math.e) / math.sqrt(D)
START = -1e30
HIDDEN = -2e30

A_BT = (((1,), (1,)), ((), ()))


def dot(a, b):
    return jnp.dot(a, b, preferred_element_type=F32)


def three(a):
    high = a.astype(BF16)
    rest = a - high.astype(F32)
    middle = rest.astype(BF16)
    low = (rest - middle.astype(F32)).astype(BF16)
    at = lax.broadcasted_iota(jnp.int32, (16, D), 0)
    rows = [jnp.broadcast_to(p[0:1].astype(F32), (16, D)) for p in (high, middle, low)]
    out = jnp.where(at == 0, rows[0], jnp.where(at == 1, rows[1], jnp.where(at == 2, rows[2], 0.0)))
    return out.astype(BF16)


def whole(part):
    part = part.astype(F32)
    return part[0:1] + part[1:2] + part[2:3]


def split(a):
    high = a.astype(BF16)
    return high, (a - high.astype(F32)).astype(BF16)


def kernel(
    lq_in, lk_in, lv_in, ld_in, sq, sk_in, sv_in, lin_out, soft_out,
    lq, lk, lv, ld, sv, in_sem, kb, vb, qb, acc, mx, ob, ls, orv, lrv,
    mixed, cums, p1s, p1r, tot, before, p2s, p2r, p3s, p3r, ssr,
    k_rs, v_rs, k_ss, v_ss, q_rs, q_ss, o_rs, o_ss, l_rs, l_ss,
    p1_rs, p1_ss, p2_rs, p2_ss, p3_rs, p3_ss, s_rs, s_ss,
):
    c = lax.axis_index("ctx")
    hd = lax.axis_index("head")
    z = c // NX
    x = c % NX

    def at_z(dz):
        return (lax.rem(z + dz + NZ, NZ) * NX + x, hd)

    def at_x(dx):
        return (z * NX + lax.rem(x + dx + NX, NX), hd)

    def at_h(dh):
        return (c, lax.rem(hd + dh, 8))

    def rows(r):
        return pl.ds(pl.multiple_of(r * R, R), R)

    def row_of(dz):
        return lax.rem(z + dz + NZ, NZ)

    def remote(src, dst, ss, rs, dev):
        return pltpu.make_async_remote_copy(
            src_ref=src, dst_ref=dst, send_sem=ss, recv_sem=rs, device_id=dev, device_id_type=MESH
        )

    def k_copy(dz, way):
        r = row_of(dz)
        n = 0 if dz == 0 and way > 0 else (1 if dz == 0 else (1 + abs(dz) if way > 0 else 4 + abs(dz)))
        return remote(kb.at[rows(r), :], kb.at[rows(r), :], k_ss.at[n], k_rs.at[r], at_z(way))

    def v_copy(dz, way):
        r = row_of(dz)
        n = 0 if dz == 0 and way > 0 else (1 if dz == 0 else (1 + abs(dz) if way > 0 else 4 + abs(dz)))
        part = vb.at[pl.ds(0, D), rows(r)]
        return remote(part, part, v_ss.at[n], v_rs.at[r], at_z(way))

    k_sends = [(0, 1), (0, -1), (-1, 1), (1, -1), (-2, 1), (2, -1), (-3, 1)]
    v_sends = [(0, 1), (0, -1), (-1, 1), (1, -1), (-2, 1), (2, -1), (3, -1)]

    def tile_of(slot, h):
        return (h, 4 + 2 * ((h + 2) % 4), 5 + 2 * h, 12 + h)[slot]

    def q_copy(slot, h):
        t = tile_of(slot, h)
        if slot < 3:
            src, dx = sq.at[:, pl.ds(h * D, D)], (-1 if slot == 1 else 1)
        elif h < 2:
            src, dx = qb.at[tile_of(2, h)], 1
        else:
            src, dx = qb.at[tile_of(1, h)], -1
        return remote(src, qb.at[t], q_ss.at[t - 4], q_rs.at[t - 4], at_x(dx))

    def o_copy(slot, h):
        dx = (1 if h == 0 else -1) if slot == 3 else (1 if slot == 1 else -1)
        part = pl.ds(h, 2)
        n = 2 * (slot - 1) + h // 2
        return remote(
            ob.at[slot - 1, part], orv.at[slot - 1, part], o_ss.at[n], o_rs.at[n], at_x(dx)
        )

    def l_copy(n):
        dx = (1, -1, 1, -1)[n]
        return remote(ls.at[min(n, 2)], lrv.at[n], l_ss.at[n], l_rs.at[n], at_x(dx))

    def p1_copy(dx):
        there = lax.rem(x + dx, NX)
        return remote(p1s.at[there], p1r.at[x], p1_ss.at[dx], p1_rs.at[x], at_x(dx))

    def p1_wait(dx):
        there = lax.rem(x + dx, NX)
        remote(p1s.at[there], p1r.at[there], p1_ss.at[dx], p1_rs.at[there], at_x(dx)).wait_recv()

    def p2_copy(n, dz):
        return remote(p2s.at[n], p2r.at[n], p2_ss.at[n, dz], p2_rs.at[n], at_z(dz))

    def p2_sends(n):
        return (z % 2 == 0, z % 4 == 1, z == 3)[n]

    def p3_copy(dx):
        there = lax.rem(x + dx, NX)
        return remote(p3s.at[there], p3r.at[x], p3_ss.at[dx], p3_rs.at[x], at_x(dx))

    def p3_wait(dx):
        there = lax.rem(x + dx, NX)
        remote(p3s.at[there], p3r.at[there], p3_ss.at[dx], p3_rs.at[there], at_x(dx)).wait_recv()

    def s_copy(dh):
        return remote(ssr.at[hd], ssr.at[hd], s_ss.at[dh], s_rs.at[hd], at_h(dh))

    def s_wait(dh):
        there = lax.rem(hd + dh, 8)
        remote(ssr.at[there], ssr.at[there], s_ss.at[dh], s_rs.at[there], at_h(dh)).wait_recv()

    places = [(sk_in, kb.at[rows(z), :]), (sv_in, sv), (ld_in, ld), (lk_in, lk), (lv_in, lv), (lq_in, lq)]
    places += [(sq.at[:, pl.ds(h * D, D)], qb.at[h]) for h in range(NH)]
    loads = [pltpu.make_async_copy(a, b, in_sem.at[n]) for n, (a, b) in enumerate(places)]
    for load in loads:
        load.start()
    barrier = pltpu.get_barrier_semaphore()
    for dz in range(1, NZ):
        pl.semaphore_signal(barrier, inc=1, device_id=at_z(dz), device_id_type=MESH)
    for dx in range(1, NX):
        pl.semaphore_signal(barrier, inc=1, device_id=at_x(dx), device_id_type=MESH)
    for dh in range(1, 8):
        pl.semaphore_signal(barrier, inc=1, device_id=at_h(dh), device_id_type=MESH)

    vb[pl.ds(D, 16), :] = jnp.ones((16, NZ * R), BF16)
    loads[1].wait()
    vb[pl.ds(0, D), rows(z)] = sv[...].T
    loads[0].wait()
    pl.semaphore_wait(barrier, 17)

    for way in (1, -1):
        k_copy(0, way).start()
        v_copy(0, way).start()
    q_copy(1, 2).start()
    q_copy(2, 0).start()

    t_at = lax.broadcasted_iota(jnp.int32, (R, R), 0)
    s_at = lax.broadcasted_iota(jnp.int32, (R, R), 1)
    causal = t_at >= s_at
    loads[2].wait()
    decay = jnp.concatenate([ld[...], jnp.zeros((D - NH, R), F32)], axis=0)
    cum_row = lax.dot_general(
        decay, causal.astype(F32), A_BT, precision=HIGHEST, preferred_element_type=F32
    )
    cum = cum_row.T
    cums[...] = cum
    for n in (3, 4):
        loads[n].wait()
    for h in range(NH):
        cols = slice(h * D, (h + 1) * D)
        kh, vh = lk[:, cols], lv[:, cols]
        last = cum[R - 1 : R, h : h + 1]
        high, low = split(kh.astype(F32) * jnp.exp(cum[:, h : h + 1] - last))
        p1s[h, 0:D, :] = (dot(high.T, vh) + dot(low.T, vh)).astype(BF16)
        p1s[h, D : D + 16, :] = three(jnp.broadcast_to(last, (8, D)))
    for dx in range(1, NX):
        p1_copy(dx).start()
    p1r[x] = p1s[x]
    q_copy(1, 3).start()
    q_copy(2, 1).start()
    for h in (0, 1):
        q_copy(1, h).start()
        q_copy(2, h + 2).start()
    loads[5].wait()
    for h in range(NH):
        cols = slice(h * D, (h + 1) * D)
        qh, kh, vh = lq[:, cols], lk[:, cols], lv[:, cols]
        spread = cum[:, h : h + 1] - cum_row[h : h + 1, :]
        scores = lax.dot_general(qh, kh, A_BT, preferred_element_type=F32)
        weights = jnp.where(causal, scores * jnp.exp(-jnp.maximum(spread, 0.0)), 0.0)
        mixed[:, cols] = dot(weights.astype(BF16), vh)

    for_all = jnp.full((8, R), START, F32)
    for t in range(16):
        mx[t] = for_all
        acc[t] = jnp.zeros((D + 16, R), F32)

    diff = s_at - t_at

    def block(i, base, size, masked):
        sub = 768 if size == 768 else 512
        parts = size // sub

        def score(j):
            q = qb[4 * i + j]
            out = []
            for n in range(parts):
                keys = kb[pl.ds(pl.multiple_of(base + n * sub, R if sub == 768 else D), sub), :]
                out.append(lax.dot_general(keys, q, A_BT, preferred_element_type=F32))
            return out

        def finish(j, ps, al):
            total = acc[4 * i + j] * al
            for n in range(parts):
                values = vb[:, pl.ds(pl.multiple_of(base + n * sub, D), sub)]
                total = total + dot(values, ps[n])
            acc[4 * i + j] = total

        now = score(0)
        pending = None
        for j in range(4):
            later = score(j + 1) if j < 3 else None
            if pending is not None:
                finish(*pending)
            if masked:
                dx = jnp.where(i == 0, 0, jnp.where(i == 3, 2, 1 if j % 2 == 0 else -1))
                there = lax.rem(x + dx + NX, NX)
                first = base // R
                halves = []
                for half in range(2):
                    lead = (NX * (z - first - half) + there - x) * R
                    seen = diff + lead >= 0
                    halves.append(jnp.where(seen, now[0][half * R : (half + 1) * R], HIDDEN))
                now = halves
            top = now[0].max(axis=0, keepdims=True)
            for n in range(1, len(now)):
                top = jnp.maximum(top, now[n].max(axis=0, keepdims=True))
            old = mx[4 * i + j, 0:1, :]
            new = jnp.maximum(old, top * SCALE)
            al = jnp.exp2(old - new)
            mx[4 * i + j, 0:1, :] = new
            ps = [jnp.exp2(s * SCALE - new).astype(BF16) for s in now]
            if masked:
                ps = [jnp.concatenate(ps, axis=0)]
            pending = (j, ps, al)
            now = later
        finish(*pending)

    def closed(t):
        l = jnp.maximum(acc[t, D : D + 1, :], 1e-35)
        return acc[t, 0:D, :] / l, mx[t, 0:1, :] + jnp.log2(l)

    def close(slot, heads, part=None):
        for h in heads:
            o, lse = closed(tile_of(slot, h))
            if part is not None:
                other = lrv[part, h : h + 1, :]
                top = jnp.maximum(lse, other)
                w, v = jnp.exp2(lse - top), jnp.exp2(other - top)
                o = (o * w + orv[2, h].astype(F32) * v) / (w + v)
                lse = top + jnp.log2(w + v)
            ob[slot - 1, h] = o.astype(BF16)
            ls[slot - 1, h : h + 1, :] = lse

    def lin_totals():
        for dx in range(1, NX):
            p1_wait(dx)
        total = p1r[0, 0:D, :].astype(F32)
        lead = whole(p1r[0, D : D + 16, :])
        for n in range(1, NX):
            g = whole(p1r[n, D : D + 16, :])
            total = total * jnp.exp(-g) + p1r[n, 0:D, :].astype(F32)
            lead = lead + g
        tot[0:D, :] = total
        tot[D : D + 8, :] = jnp.broadcast_to(lead, (8, D))
        before[...] = jnp.zeros((D + 8, D), F32)
        lin_send(0)

    def lin_send(n):
        @pl.when(p2_sends(n))
        def _():
            g = tot[D : D + 8, :]
            p2s[n, 0:D, :] = before[0:D, :] * jnp.exp(-g[0:1]) + tot[0:D, :]
            p2s[n, D : D + 8, :] = before[D : D + 8, :] + g
            for dz in range(1, 2**n + 1):
                p2_copy(n, dz).start()

    def lin_get(n):
        @pl.when((z % 2 == 1, z % 4 >= 2, z >= 4)[n])
        def _():
            p2_copy(n, 1).wait_recv()
            lead = before[D : D + 8, :]
            before[0:D, :] = p2r[n, 0:D, :] * jnp.exp(-lead[0:1]) + before[0:D, :]
            before[D : D + 8, :] = lead + p2r[n, D : D + 8, :]

    def lin_prefix():
        lin_get(2)
        state = before[0:D, :]
        p3s[0] = state.astype(BF16)
        for n in range(1, NX):
            g = whole(p1r[n - 1, D : D + 16, :])
            state = state * jnp.exp(-g) + p1r[n - 1, 0:D, :].astype(F32)
            p3s[n] = state.astype(BF16)
        for dx in range(1, NX):
            p3_copy(dx).start()
        p3r[x] = p3s[x]

    def lin_mix():
        for dx in range(1, NX):
            p3_wait(dx)
        square = jnp.zeros((R, D), F32)
        for h in range(NH):
            cols = slice(h * D, (h + 1) * D)
            inter = dot(lq[:, cols], p3r[h])
            m = mixed[:, cols] + jnp.exp(-cums[:, h : h + 1]) * inter
            mixed[:, cols] = m
            square = square + m * m
        ssr[hd] = lax.dot_general(
            jnp.ones((8, D), F32), square, A_BT, precision=HIGHEST, preferred_element_type=F32
        )
        for dh in range(1, 8):
            s_copy(dh).start()

    def z_step(d):
        for wait, copy, sends in ((wait_k, k_copy, k_sends), (wait_v, v_copy, v_sends)):
            for dz in (-d, d) if d < 4 else (4,):
                wait(dz)
                for there, way in sends:
                    if there == dz:
                        copy(dz, way).start()

    def wait_k(dz):
        r = row_of(dz)
        part = kb.at[rows(r), :]
        remote(part, part, k_ss.at[0], k_rs.at[r], at_z(1)).wait_recv()

    def wait_v(dz):
        r = row_of(dz)
        part = vb.at[pl.ds(0, D), rows(r)]
        remote(part, part, v_ss.at[0], v_rs.at[r], at_z(1)).wait_recv()

    own = 2 * (z // 2) * R

    def step(n, carry):
        is_a = (n <= 1) | (n == 3) | (n == 5)
        is_b = (n == 2) | (n == 4) | (n == 6) | (n == 10)
        is_c = ((n >= 7) & (n <= 9)) | (n == 11)
        i = jnp.where((n == 0) | (n >= 10), 0, jnp.where((n == 1) | (n == 2) | (n == 8), 1, 3))
        i = jnp.where((n == 3) | (n == 4) | (n == 9), 2, i)

        @pl.when(n == 0)
        def _():
            z_step(1)
            for load in loads[6:]:
                load.wait()

        @pl.when(n == 1)
        def _():
            for h in (0, 1):
                q_copy(2, h).wait_recv()
                q_copy(3, h).start()
                q_copy(1, h + 2).wait_recv()
                q_copy(3, h + 2).start()

        @pl.when(n == 2)
        def _():
            z_step(2)

        @pl.when(n == 3)
        def _():
            for h in (0, 1):
                q_copy(1, h).wait_recv()
                q_copy(2, h + 2).wait_recv()
            lin_totals()

        @pl.when(n == 4)
        def _():
            lin_get(0)
            lin_send(1)

        @pl.when(n == 5)
        def _():
            z_step(3)
            for h in range(NH):
                q_copy(3, h).wait_recv()

        @pl.when(n == 6)
        def _():
            lin_get(1)
            lin_send(2)

        @pl.when(n == 7)
        def _():
            z_step(4)

        @pl.when(n == 8)
        def _():
            lin_prefix()

        @pl.when(n == 10)
        def _():
            lin_mix()

        @pl.when(is_a)
        def _():
            block(i, own, 768, True)

        @pl.when(is_b & ((z == 7) | ((z % 2 == 0) & (z > 0))))
        def _():
            block(i, jnp.where(z == 7, 0, (z - 2) * R), 768, False)

        @pl.when(is_c & (z >= 5))
        def _():
            block(i, jnp.where(z == 7, 2 * R, 0), 1536, False)

        @pl.when(is_c & ((z == 3) | (z == 4)))
        def _():
            block(i, 0 * z, 768, False)

        @pl.when(n == 7)
        def _():
            close(3, range(NH))
            for m in (2, 3):
                l_copy(m).start()
            for h in (0, 2):
                o_copy(3, h).start()

        @pl.when(n == 8)
        def _():
            for slot, h in ((1, 2), (2, 0)):
                close(slot, (h, h + 1))
                o_copy(slot, h).start()

        @pl.when(n == 9)
        def _():
            for m, slot, h in ((2, 1, 0), (3, 2, 2)):
                l_copy(m).wait_recv()
                o_copy(3, h).wait_recv()
                close(slot, (h, h + 1), m)
                l_copy(slot - 1).start()
                o_copy(slot, h).start()

        return carry

    lax.fori_loop(0, 12, step, 0)

    for dh in range(1, 8):
        s_wait(dh)
    square = ssr[0]
    for n in range(1, 8):
        square = square + ssr[n]
    scale = lax.rsqrt(square[0:1, :] * (1.0 / MODEL) + 1e-05)
    scale = jnp.broadcast_to(scale, (D, R)).T
    for h in range(NH):
        cols = slice(h * D, (h + 1) * D)
        lin_out[:, cols] = mixed[:, cols] * scale

    for m in (0, 1):
        l_copy(m).wait_recv()
    for slot, h in ((1, 2), (2, 0), (1, 0), (2, 2)):
        o_copy(slot, h).wait_recv()
    for h in range(NH):
        o, lse = closed(h)
        others = [lrv[n, h : h + 1, :] for n in range(2)]
        top = jnp.maximum(lse, jnp.maximum(*others))
        w = jnp.exp2(lse - top)
        total = w
        o = o * w
        for n in range(2):
            w = jnp.exp2(others[n] - top)
            total = total + w
            o = o + orv[n, h].astype(F32) * w
        soft_out[:, h * D : (h + 1) * D] = (o / total).T

    for dz, way in k_sends:
        k_copy(dz, way).wait_send()
    for dz, way in v_sends:
        v_copy(dz, way).wait_send()
    for slot in (1, 2, 3):
        for h in range(NH):
            q_copy(slot, h).wait_send()
        for h in (0, 2):
            o_copy(slot, h).wait_send()
    for m in range(4):
        l_copy(m).wait_send()
    for dx in range(1, NX):
        p1_copy(dx).wait_send()
        p3_copy(dx).wait_send()
    for n in range(3):
        @pl.when(p2_sends(n))
        def _():
            for dz in range(1, 2**n + 1):
                p2_copy(n, dz).wait_send()
    for dh in range(1, 8):
        s_copy(dh).wait_send()


def body(lin_q, lin_k, lin_v, lin_decay, soft_q, soft_k, soft_v):
    dma = pltpu.SemaphoreType.DMA
    vmem = pl.BlockSpec(memory_space=pltpu.VMEM)
    out = jax.ShapeDtypeStruct((R, NH * D), F32)
    return pl.pallas_call(
        kernel,
        out_shape=(out, out),
        in_specs=[pl.BlockSpec(memory_space=pl.ANY)] * 7,
        out_specs=(vmem, vmem),
        scratch_shapes=[
            pltpu.VMEM((R, NH * D), BF16),
            pltpu.VMEM((R, NH * D), BF16),
            pltpu.VMEM((R, NH * D), BF16),
            pltpu.VMEM((NH, R), F32),
            pltpu.VMEM((R, D), BF16),
            dma((10,)),
            pltpu.VMEM((NZ * R, D), BF16),
            pltpu.VMEM((D + 16, NZ * R), BF16),
            pltpu.VMEM((16, R, D), BF16),
            pltpu.VMEM((16, D + 16, R), F32),
            pltpu.VMEM((16, 8, R), F32),
            pltpu.VMEM((3, NH, D, R), BF16),
            pltpu.VMEM((3, 8, R), F32),
            pltpu.VMEM((3, NH, D, R), BF16),
            pltpu.VMEM((4, 8, R), F32),
            pltpu.VMEM((R, NH * D), F32),
            pltpu.VMEM((R, D), F32),
            pltpu.VMEM((NX, D + 16, D), BF16),
            pltpu.VMEM((NX, D + 16, D), BF16),
            pltpu.VMEM((D + 8, D), F32),
            pltpu.VMEM((D + 8, D), F32),
            pltpu.VMEM((3, D + 8, D), F32),
            pltpu.VMEM((3, D + 8, D), F32),
            pltpu.VMEM((NX, D, D), BF16),
            pltpu.VMEM((NX, D, D), BF16),
            pltpu.VMEM((8, 8, R), F32),
            dma((8,)), dma((8,)), dma((8,)), dma((8,)),
            dma((12,)), dma((12,)), dma((6,)), dma((6,)), dma((4,)), dma((4,)),
            dma((4,)), dma((4,)), dma((3,)), dma((3, 5)), dma((4,)), dma((4,)), dma((8,)), dma((8,)),
        ],
        compiler_params=pltpu.CompilerParams(
            collective_id=0, has_side_effects=True, vmem_limit_bytes=56 << 20
        ),
    )(lin_q, lin_k, lin_v, lin_decay.T, soft_q, soft_k, soft_v)


def solution(mesh):
    spec = P("ctx", "head")
    return jax.shard_map(
        body, mesh=mesh, in_specs=(spec,) * 7, out_specs=(spec, spec), check_vma=False
    )
```

time: 78.5 us -> 54.9 us (0.70)
  Pallas kernels: 70.5 us -> 51.1 us
  local copies, waits for them, and re-layouts: 6.67 us -> 3.02 us
    pallas_call x1, Pallas kernels: 70.5 us -> 51.1 us  [body(): pl.pallas_call(kernel, out_shape=(out, out), in_specs=[pl.BlockSpec(memor...]
    unnamed x15 -> x4, local copies, waits for them, and re-layouts: 6.67 us -> 3.02 us
where the time goes in v2:
time: 54.9 us; the launch traced here: 54.8 us
  Pallas kernels  51.1 us (93%)
  local copies, waits for them, and re-layouts  3.02 us (6%)
  between operations  0.65 us (1%)
    pallas_call x1, Pallas kernels, body(): pl.pallas_call(kernel, out_shape=(out, out), in_specs=[pl.BlockSpec(memor...  51.1 us
    unnamed x4, local copies, waits for them, and re-layouts  3.02 us

profile of v2, /device:TPU:224, one launch (start us, length us, event | category | flops | bytes accessed | tf_op | source)
XLA Modules:
  0.0 54.8 jit_solution(14338583633278157371)
XLA Ops:
  0.6 51.1 %shard_map.86 = (f32[384,512]{1,0:T(8,128)}, f32[384,512]{1,0:T(8,128)}) custom-call(bf16[384,512]{1,0:T(8,128)(2,1)} %lq_in.1, bf16[384,512]{1,0:T(8,128)(2,1)} %lk_in.1, bf16[384,512]{1,0:T(8,128)(2,1)} %lv_in.1, f32[4,384]{1,0:T(4,128)} %bitcast.1, bf16[384,512]{1,0:T(8,128)(2,1)} %sq.1, bf16[384,128]{1,0:T(8,128)(2,1)} %sk_in.1, bf16[384,128]{1,0:T(8,128)(2,1)} %sv_in.1), custom_call_target="tpu_custom_call" | custom-call | tf_op jit(solution)/shard_map/pallas_call | solution.py:522
  51.7 0.0 copy-start
  51.7 2.1 %copy.11 = f32[384,512]{1,0:T(8,128)} copy(f32[384,512]{1,0:T(8,128)} %get-tuple-element.4) | data formatting | bytes 1572864
  53.9 0.0 copy-done
  53.9 0.9 %copy.12 = f32[384,512]{1,0:T(8,128)} copy(f32[384,512]{1,0:T(8,128)S(1)} %copy-done) | data formatting | bytes 1572864
Async XLA Ops:
  51.7 2.1 %copy-start = (f32[384,512]{1,0:T(8,128)S(1)}, f32[384,512]{1,0:T(8,128)}, u32[]{:S(2)}) copy-start(f32[384,512]{1,0:T(8,128)} %get-tuple-element.5) | copy-start | bytes 2359300

commit v3 on v2

--- a/solution.py
+++ b/solution.py
@@ -51,7 +51,7 @@
 
 def kernel(
     lq_in, lk_in, lv_in, ld_in, sq, sk_in, sv_in, lin_out, soft_out,
-    lq, lk, lv, ld, sv, in_sem, kb, vb, qb, acc, mx, ob, ls, orv, lrv,
+    lq, lk, lv, ld, sv, in_sem, so, out_sem, kb, vb, qb, acc, mx, ob, ls, orv, lrv,
     mixed, cums, p1s, p1r, tot, before, p2s, p2r, p3s, p3r, ssr,
     k_rs, v_rs, k_ss, v_ss, q_rs, q_ss, o_rs, o_ss, l_rs, l_ss,
     p1_rs, p1_ss, p2_rs, p2_ss, p3_rs, p3_ss, s_rs, s_ss,
@@ -473,7 +473,9 @@
     scale = jnp.broadcast_to(scale, (D, R)).T
     for h in range(NH):
         cols = slice(h * D, (h + 1) * D)
-        lin_out[:, cols] = mixed[:, cols] * scale
+        mixed[:, cols] = mixed[:, cols] * scale
+    stores = [pltpu.make_async_copy(mixed, lin_out, out_sem.at[NH])]
+    stores[0].start()
 
     for m in (0, 1):
         l_copy(m).wait_recv()
@@ -490,7 +492,10 @@
             w = jnp.exp2(others[n] - top)
             total = total + w
             o = o + orv[n, h].astype(F32) * w
-        soft_out[:, h * D : (h + 1) * D] = (o / total).T
+        cols = pl.ds(h * D, D)
+        so[h] = (o / total).T
+        stores.append(pltpu.make_async_copy(so.at[h], soft_out.at[:, cols], out_sem.at[h]))
+        stores[-1].start()
 
     for dz, way in k_sends:
         k_copy(dz, way).wait_send()
@@ -514,16 +519,17 @@
     for dh in range(1, 8):
         s_copy(dh).wait_send()
 
+    for store in stores:
+        store.wait()
 
 def body(lin_q, lin_k, lin_v, lin_decay, soft_q, soft_k, soft_v):
     dma = pltpu.SemaphoreType.DMA
-    vmem = pl.BlockSpec(memory_space=pltpu.VMEM)
     out = jax.ShapeDtypeStruct((R, NH * D), F32)
     return pl.pallas_call(
         kernel,
         out_shape=(out, out),
         in_specs=[pl.BlockSpec(memory_space=pl.ANY)] * 7,
-        out_specs=(vmem, vmem),
+        out_specs=(pl.BlockSpec(memory_space=pl.ANY),) * 2,
         scratch_shapes=[
             pltpu.VMEM((R, NH * D), BF16),
             pltpu.VMEM((R, NH * D), BF16),
@@ -531,6 +537,8 @@
             pltpu.VMEM((NH, R), F32),
             pltpu.VMEM((R, D), BF16),
             dma((10,)),
+            pltpu.VMEM((NH, R, D), F32),
+            dma((NH + 1,)),
             pltpu.VMEM((NZ * R, D), BF16),
             pltpu.VMEM((D + 16, NZ * R), BF16),
             pltpu.VMEM((16, R, D), BF16),

time: 54.9 us -> 54.5 us (level)
  no operation moved by 1% of the time
where the time goes in v3:
time: 54.5 us; the launch traced here: 54.4 us
  Pallas kernels  50.7 us (93%)
  local copies, waits for them, and re-layouts  3.02 us (6%)
  between operations  0.65 us (1%)
    pallas_call x1, Pallas kernels, body(): pl.pallas_call(kernel, out_shape=(out, out), in_specs=[pl.BlockSpec(memor...  50.7 us
    unnamed x4, local copies, waits for them, and re-layouts  3.02 us

profile of v3, /device:TPU:224, one launch (start us, length us, event | category | flops | bytes accessed | tf_op | source)
XLA Modules:
  0.0 54.4 jit_solution(8412741265536888299)
XLA Ops:
  0.6 50.7 %shard_map.86 = (f32[384,512]{1,0:T(8,128)}, f32[384,512]{1,0:T(8,128)}) custom-call(bf16[384,512]{1,0:T(8,128)(2,1)} %lq_in.1, bf16[384,512]{1,0:T(8,128)(2,1)} %lk_in.1, bf16[384,512]{1,0:T(8,128)(2,1)} %lv_in.1, f32[4,384]{1,0:T(4,128)} %bitcast.1, bf16[384,512]{1,0:T(8,128)(2,1)} %sq.1, bf16[384,128]{1,0:T(8,128)(2,1)} %sk_in.1, bf16[384,128]{1,0:T(8,128)(2,1)} %sv_in.1), custom_call_target="tpu_custom_call" | custom-call | tf_op jit(solution)/shard_map/pallas_call | solution.py:528
  51.3 0.0 copy-start
  51.4 2.1 %copy.11 = f32[384,512]{1,0:T(8,128)} copy(f32[384,512]{1,0:T(8,128)} %get-tuple-element.4) | data formatting | bytes 1572864
  53.5 0.0 copy-done
  53.5 0.9 %copy.12 = f32[384,512]{1,0:T(8,128)} copy(f32[384,512]{1,0:T(8,128)S(1)} %copy-done) | data formatting | bytes 1572864
Async XLA Ops:
  51.3 2.1 %copy-start = (f32[384,512]{1,0:T(8,128)S(1)}, f32[384,512]{1,0:T(8,128)}, u32[]{:S(2)}) copy-start(f32[384,512]{1,0:T(8,128)} %get-tuple-element.5) | copy-start | bytes 2359300

commit v4 on v3

--- a/solution.py
+++ b/solution.py
@@ -417,7 +417,7 @@
         def _():
             lin_prefix()
 
-        @pl.when(n == 10)
+        @pl.when(n == 11)
         def _():
             lin_mix()
 

time: 54.5 us -> 55.5 us (1.018)
  the two profiles are of different devices: /device:TPU:224 before, /device:TPU:193 now
where the time goes in v4:
time: 55.5 us; the launch traced here: 55.4 us
  Pallas kernels  51.7 us (93%)
  local copies, waits for them, and re-layouts  3.02 us (5%)
  between operations  0.65 us (1%)
    pallas_call x1, Pallas kernels, body(): pl.pallas_call(kernel, out_shape=(out, out), in_specs=[pl.BlockSpec(memor...  51.7 us
    unnamed x4, local copies, waits for them, and re-layouts  3.02 us

profile of v4, /device:TPU:193, one launch (start us, length us, event | category | flops | bytes accessed | tf_op | source)
XLA Modules:
  0.0 55.4 jit_solution(1919442544463409048)
XLA Ops:
  0.6 51.7 %shard_map.86 = (f32[384,512]{1,0:T(8,128)}, f32[384,512]{1,0:T(8,128)}) custom-call(bf16[384,512]{1,0:T(8,128)(2,1)} %lq_in.1, bf16[384,512]{1,0:T(8,128)(2,1)} %lk_in.1, bf16[384,512]{1,0:T(8,128)(2,1)} %lv_in.1, f32[4,384]{1,0:T(4,128)} %bitcast.1, bf16[384,512]{1,0:T(8,128)(2,1)} %sq.1, bf16[384,128]{1,0:T(8,128)(2,1)} %sk_in.1, bf16[384,128]{1,0:T(8,128)(2,1)} %sv_in.1), custom_call_target="tpu_custom_call" | custom-call | tf_op jit(solution)/shard_map/pallas_call | solution.py:528
  52.3 0.0 copy-start
  52.4 2.1 %copy.11 = f32[384,512]{1,0:T(8,128)} copy(f32[384,512]{1,0:T(8,128)} %get-tuple-element.4) | data formatting | bytes 1572864
  54.5 0.0 copy-done
  54.5 0.9 %copy.12 = f32[384,512]{1,0:T(8,128)} copy(f32[384,512]{1,0:T(8,128)S(1)} %copy-done) | data formatting | bytes 1572864
Async XLA Ops:
  52.3 2.1 %copy-start = (f32[384,512]{1,0:T(8,128)S(1)}, f32[384,512]{1,0:T(8,128)}, u32[]{:S(2)}) copy-start(f32[384,512]{1,0:T(8,128)} %get-tuple-element.5) | copy-start | bytes 2359300
